TPU v7x, 256 devices: a whole 4x4x8 slice. The times are simulated.
256 devices in a mesh: seq: 64 (over z, y, x_lo), head: 4 (over x_hi, core).
Axes of the slice: x: 4 (x_hi: 2, x_lo: 2; x = x_hi * 2 + x_lo), y: 4, z: 8, core: 2. Of those that a mesh axis runs over, the one named last changes fastest.
Arguments:
- queries: bfloat16 [8192, 8192], P(('seq', 'head')), may hold values from -20 to 20
- keys: bfloat16 [8192, 1024], P(('seq', 'head')), may hold values from -8 to 8
- values: bfloat16 [8192, 1024], P(('seq', 'head')), may hold values from -6 to 6
Outputs:
- attended: bfloat16 [8192, 8192], P(('seq', 'head'))
All inputs are finite; a program needn't handle non-finite values.
Results may differ from a plain program's by a relative error of at most 0.0059.
Values may be sent and summed in bfloat16 or wider, within the bound.
A program may use at most 64 MiB of HBM per device.

v0:
```python
import math

import jax
import jax.numpy as jnp
from jax import lax
from jax.sharding import PartitionSpec as P

HEAD_DIM = 128


def arrange_queries(query_half, kv_here, group):
    half_rows = query_half.shape[0]
    grid = query_half.reshape(half_rows, kv_here, group, HEAD_DIM)
    return jnp.transpose(grid, (1, 2, 0, 3)).reshape(kv_here, group * half_rows, HEAD_DIM)


def attend(state, query_grid, query_pos, key_block, value_block, key_start):
    running_top, running_total, accum = state
    block = key_block.shape[0]
    kv_here = query_grid.shape[0]
    key_grid = jnp.transpose(key_block.reshape(block, kv_here, HEAD_DIM), (1, 0, 2))
    value_grid = jnp.transpose(value_block.reshape(block, kv_here, HEAD_DIM), (1, 0, 2))
    score = jnp.einsum(
        "gqd,gkd->gqk", query_grid, key_grid, preferred_element_type=jnp.float32
    ) * HEAD_DIM ** (-0.5)
    key_pos = key_start + jnp.arange(block, dtype=jnp.int32)
    score = jnp.where(query_pos[None, :, None] >= key_pos[None, None, :], score, -jnp.inf)
    new_top = jnp.maximum(running_top, jnp.max(score, axis=2))
    rescale = jnp.exp(running_top - new_top)
    weight = jnp.exp(score - new_top[:, :, None])
    new_total = running_total * rescale + jnp.sum(weight, axis=2)
    mixed = jnp.einsum(
        "gqk,gkd->gqd", weight.astype(jnp.bfloat16), value_grid, preferred_element_type=jnp.float32
    )
    return (new_top, new_total, accum * rescale[:, :, None] + mixed)


def sweep_piece(state, query_grid, query_pos, last_pos, key_piece, value_piece):
    piece_rows = key_piece.shape[0]
    block = math.gcd(piece_rows, 512)

    def advance(step, current):
        offset = step * block
        key_block = lax.dynamic_slice_in_dim(key_piece, offset, block, 0)
        value_block = lax.dynamic_slice_in_dim(value_piece, offset, block, 0)
        return lax.cond(
            offset <= last_pos,
            lambda inner: attend(inner, query_grid, query_pos, key_block, value_block, offset),
            lambda inner: inner,
            current,
        )

    return lax.fori_loop(0, piece_rows // block, advance, state)


def empty_state(kv_here, width):
    return (
        jnp.full((kv_here, width), -1e30, jnp.float32),
        jnp.zeros((kv_here, width), jnp.float32),
        jnp.zeros((kv_here, width, HEAD_DIM), jnp.float32),
    )


def finish(state, kv_here, group, half_rows):
    running_top, running_total, accum = state
    output = accum / running_total[:, :, None]
    output = output.reshape(kv_here, group, half_rows, HEAD_DIM)
    output = jnp.transpose(output, (2, 0, 1, 3)).reshape(half_rows, kv_here * group * HEAD_DIM)
    return output.astype(jnp.bfloat16)


def on_device(queries, keys, values):
    query_rows, key_rows, value_rows = (
        lax.all_to_all(queries, "head", split_axis=1, concat_axis=0, tiled=True),
        lax.all_to_all(keys, "head", split_axis=1, concat_axis=0, tiled=True),
        lax.all_to_all(values, "head", split_axis=1, concat_axis=0, tiled=True),
    )
    slab = query_rows.shape[0]
    half_rows = slab // 2
    kv_here = key_rows.shape[1] // HEAD_DIM
    group = query_rows.shape[1] // HEAD_DIM // kv_here
    own = lax.axis_index("seq")
    later = query_rows[half_rows:]
    later_start = own * slab + half_rows
    first_start = own * slab
    grids = (
        arrange_queries(query_rows[:half_rows], kv_here, group),
        arrange_queries(later, kv_here, group),
    )
    local_pos = jnp.arange(group * half_rows, dtype=jnp.int32) % half_rows
    positions = (first_start + local_pos, later_start + local_pos)
    lasts = (first_start + half_rows - 1, later_start + half_rows - 1)
    width = group * half_rows
    initial = (empty_state(kv_here, width), empty_state(kv_here, width))
    key_piece = lax.all_gather(key_rows, "seq", axis=0, tiled=True)
    value_piece = lax.all_gather(value_rows, "seq", axis=0, tiled=True)
    first = sweep_piece(initial[0], grids[0], positions[0], lasts[0], key_piece, value_piece)
    second = sweep_piece(initial[1], grids[1], positions[1], lasts[1], key_piece, value_piece)
    first_out = finish(first, kv_here, group, half_rows)
    later_out = finish(second, kv_here, group, half_rows)
    joined = jnp.concatenate([first_out, later_out], axis=0)
    return lax.all_to_all(joined, "head", split_axis=0, concat_axis=1, tiled=True)


def solution(mesh):
    in_specs = (P(("seq", "head"), None), P(("seq", "head"), None), P(("seq", "head"), None))
    out_specs = P(("seq", "head"), None)
    return jax.shard_map(
        on_device, mesh=mesh, in_specs=in_specs, out_specs=out_specs, check_vma=False
    )
```

profile of v0, /device:TPU:248, one launch (start us, length us, event | category | flops | bytes accessed | tf_op | source)
XLA Modules:
  0.0 774.6 jit_solution(16771664089673948529)
XLA Ops:
  7.4 9.8 %all_to_all.73 = bf16[32,4,256]{2,0,1:T(8,128)(2,1)} all-to-all(bf16[32,4,256]{2,0,1:T(8,128)(2,1)S(1)} %bitcast.105), channel_id=1, replica_groups=mesh['seq'=64,'head'=4] {'head'}, dimensions={1} | all-to-all | bytes 131072 | tf_op jit(solution)/shard_map/all_to_all | solution.py:75
  18.1 8.7 %all_to_all.74 = bf16[32,4,256]{2,0,1:T(8,128)(2,1)} all-to-all(bf16[32,4,256]{2,0,1:T(8,128)(2,1)S(1)} %bitcast.106), channel_id=1, replica_groups=mesh['seq'=64,'head'=4] {'head'}, dimensions={1} | all-to-all | bytes 131072 | tf_op jit(solution)/shard_map/all_to_all | solution.py:76
  28.7 3.5 all-to-all-start.1
  32.2 12.0 %all-to-all-done.1 = bf16[32,4,2048]{2,0,1:T(8,128)(2,1)S(1)} async-done(((bf16[32,4,2048]{2,0,1:T(8,128)(2,1)}), bf16[32,4,2048]{2,0,1:T(8,128)(2,1)S(1)}, u32[]{:S(2)}, u32[]{:S(2)}) %all-to-all-start.1) | async-done | bytes 524320 | tf_op jit(solution)/shard_map/all_to_all | solution.py:74
  45.2 273.4 %all-gather.3.cloned.1.call-done = bf16[8192,256]{1,0:T(8,128)(2,1)} async-done(((bf16[128,256]{1,0:T(8,128)(2,1)}), bf16[8192,256]{1,0:T(8,128)(2,1)}) %all-gather.3.cloned.1.call-update) | async-done | bytes 4194320 | tf_op jit(solution)/shard_map/all_gather | solution.py:95
  318.5 6.4 copy.63
  324.9 296.0 %all-gather.5.cloned.1.call-done = bf16[8192,256]{1,0:T(8,128)(2,1)} async-done(((bf16[128,256]{1,0:T(8,128)(2,1)}), bf16[8192,256]{1,0:T(8,128)(2,1)}) %all-gather.5.cloned.1.call-update) | async-done | bytes 4194320 | tf_op jit(solution)/shard_map/all_gather | solution.py:96
  620.9 6.4 copy.64
  627.3 68.9 %while.36 = (s32[]{:T(128)}, f32[2,512]{1,0:T(2,128)S(1)}, f32[2,512]{1,0:T(2,128)S(1)}, f32[2,512,128]{2,1,0:T(8,128)S(1)}, s32[]{:T(128)}, /*index=5*/bf16[819...) while((s32[]{:T(128)}, f32[2,512]{1,0:T(2,128)S(1)}, ...), condition=%wide.region_5.6_spmd.clone, body=%wide.region_0.5_spmd.clone.sunk | while | flops 272635904 | bytes 10836321 | solution.py:53
  627.4 4.3 conditional.6
  631.7 4.3 conditional.6
  636.0 4.3 conditional.6
  640.3 4.3 conditional.6
  644.6 4.3 conditional.6
  648.9 4.3 conditional.6
  653.2 4.3 conditional.6
  657.5 4.3 conditional.6
  661.8 4.3 conditional.6
  666.1 4.3 conditional.6
  670.4 4.3 conditional.6
  674.7 4.3 conditional.6
  679.0 4.3 conditional.6
  683.3 4.3 conditional.6
  687.6 4.3 conditional.6
  691.9 4.3 conditional.6
  697.4 53.6 %while.37 = (s32[]{:T(128)}, f32[2,512]{1,0:T(2,128)S(1)}, f32[2,512]{1,0:T(2,128)S(1)}, f32[2,512,128]{2,1,0:T(8,128)S(1)}, s32[]{:T(128)}, /*index=5*/bf16[819...) while((s32[]{:T(128)}, f32[2,512]{1,0:T(2,128)S(1)}, ...), condition=%wide.region_11.12_spmd.clone, body=%wide.region_6.11_spmd.clone.sunk | while | flops 272635904 | bytes 10836321 | solution.py:53
  697.4 3.3 conditional.7
  700.8 3.3 conditional.7
  704.1 3.3 conditional.7
  707.5 3.3 conditional.7
  710.8 3.3 conditional.7
  752.5 14.5 %all_to_all.75 = bf16[4,32,2048]{2,1,0:T(8,128)(2,1)S(1)} all-to-all(bf16[4,32,2048]{2,1,0:T(8,128)(2,1)S(1)} %bitcast.92), channel_id=1, replica_groups=mesh['seq'=64,'head'=4] {'head'}, dimensions={0} | all-to-all | bytes 1048576 | tf_op jit(solution)/shard_map/all_to_all | solution.py:102
  (452 shorter events, 162.8 us)
Async XLA Ops:
  6.5 312.0 %all-gather.3.cloned.1.call-start = ((), (), s32[]{:S(2)}) async-start(), calls=%async_computation.4 | async-start | bytes 4259840 | tf_op jit(solution)/shard_map/all_gather | solution.py:95
  17.2 603.7 %all-gather.5.cloned.1.call-start = ((), (), s32[]{:S(2)}) async-start(), calls=%async_computation.5 | async-start | bytes 4259840 | tf_op jit(solution)/shard_map/all_gather | solution.py:96
  28.7 15.5 %all-to-all-start.1 = ((bf16[32,4,2048]{2,0,1:T(8,128)(2,1)}), bf16[32,4,2048]{2,0,1:T(8,128)(2,1)S(1)}, u32[]{:S(2)}, u32[]{:S(2)}) async-start(bf16[32,4,2048]{2,0,1:T(8,128)(2,1)} %bitcast.82), calls=%async_computation.1 | async-start | bytes 1048576 | tf_op jit(solution)/shard_map/all_to_all | solution.py:74
Sparse Core Ops, SparseCore 0:
  17.3 301.1 all-gather.2
  320.3 300.5 all-gather.4
where the time goes:
time: 776 us; the launch traced here: 775 us
  waiting for transfers between devices  581 us (75%)
  local copies, waits for them, and re-layouts  65.6 us (8%)
  matrix products  55.5 us (7%)
  blocking collectives  32.9 us (4%)
  other arithmetic  18.2 us (2%)
  between operations  13.5 us (2%)
    all_gather x1, waiting for transfers between devices, on_device(): value_piece = lax.all_gather(value_rows, 'seq', axis=0, tiled=True)  296 us
    all_gather x1, waiting for transfers between devices, on_device(): key_piece = lax.all_gather(key_rows, 'seq', axis=0, tiled=True)  273 us
    dynamic_slice x32, local copies, waits for them, and re-layouts, advance(): value_block = lax.dynamic_slice_in_dim(value_piece, offset, block, 0)  34.3 us
    dot_general x32, matrix products, attend(): jnp.einsum('gqd,gkd->gqk', query_grid, key_grid, preferred_element_type=j...  33 us
    dot_general x32, matrix products, attend(): jnp.einsum('gqk,gkd->gqd', weight.astype(jnp.bfloat16), value_grid, prefe...  22.5 us
  transfers between devices with their start and end apart: 3, of which 3 were waited for; matrix products, arithmetic and copies ran while one was open for 1% of the time, Pallas kernels for 0%

commit v1 on v0

v1 whole, which is shorter than its diff:
```python
import jax
import jax.numpy as jnp
import numpy as np
from jax import lax
from jax.experimental import pallas as pl
from jax.experimental.pallas import tpu as pltpu
from jax.sharding import PartitionSpec as P

MESH = pl.DeviceIdType.MESH
HEAD_DIM = 128
GROUP = 8
WIDE = GROUP * HEAD_DIM
BLOCK = 32
PEERS = 8
ROWS = PEERS * BLOCK
PLANE = 4 * ROWS
RING = 8
SCALE = np.float32(HEAD_DIM**-0.5 / np.log(2.0))
LOW = np.float32(-1e30)
TRANSPOSED = (((1,), (1,)), ((), ()))
PIECES = 4
PIECE = WIDE // PIECES


def kernel(
    queries, keys, values, out,
    qbuf, kv, obuf, tops, sums, acc, score_a, score_b,
    local_sem, q_send, q_recv, kv_send, kv_recv, y_send, y_recv,
    ring_send, ring_recv, twin_send, twin_recv, o_send, o_recv,
):
    seq, head = lax.axis_index("seq"), lax.axis_index("head")
    x_lo, y, z = seq % 2, (seq // 2) % 4, seq // 8
    x_hi, core = head // 2, head % 2
    fold = ((y + 1) // 2) % 2
    me = (y // 2) * 4 + x_hi * 2 + x_lo

    def at(z_, y_, x_hi_, x_lo_, core_):
        return ((z_ * 4 + y_) * 2 + x_lo_, x_hi_ * 2 + core_)

    def peer(step):
        other = (me + step) % PEERS
        row = jnp.where(other >= 4, 3 - fold, fold)
        return other, at(z, row, (other % 4) // 2, other % 2, core)

    up, down = at((z + 1) % RING, y, x_hi, x_lo, core), at((z + RING - 1) % RING, y, x_hi, x_lo, core)
    beside = at(z, y + 1 - 2 * (y % 2), x_hi, x_lo, core)
    twin = at(z, y, x_hi, x_lo, 1 - core)

    barrier = pltpu.get_barrier_semaphore()
    for step in range(1, PEERS):
        pl.semaphore_signal(barrier, inc=1, device_id=peer(step)[1], device_id_type=MESH)
    for device in (up, down, beside, twin):
        pl.semaphore_signal(barrier, inc=1, device_id=device, device_id_type=MESH)
    pl.semaphore_wait(barrier, PEERS + 3)

    def part(core_, fold_):
        return pl.multiple_of((core_ * 2 + fold_) * ROWS, ROWS)

    def lanes(index, width):
        return pl.ds(pl.multiple_of(index * width, width), width)

    def remote(src, dst, send, recv, device):
        return pltpu.make_async_remote_copy(
            src_ref=src, dst_ref=dst, send_sem=send, recv_sem=recv, device_id=device, device_id_type=MESH
        )

    mine = pl.ds(pl.multiple_of(part(core, fold) + me * BLOCK, BLOCK), BLOCK)

    def kv_copy(step, which):
        other, device = peer(step)
        src = (keys, values)[which]
        return remote(
            src.at[:, lanes(other, HEAD_DIM)], kv.at[z, which, mine],
            kv_send.at[which, step], kv_recv.at[which, step], device,
        )

    def q_copy(step):
        other, device = peer(step)
        return remote(queries.at[:, lanes(other, WIDE)], qbuf.at[me], q_send.at[step], q_recv.at[step], device)

    for step in range(1, PEERS):
        for which in range(2):
            kv_copy(step, which).start()
    own = (
        pltpu.make_async_copy(keys.at[:, lanes(me, HEAD_DIM)], kv.at[z, 0, mine], local_sem.at[0]),
        pltpu.make_async_copy(values.at[:, lanes(me, HEAD_DIM)], kv.at[z, 1, mine], local_sem.at[1]),
        pltpu.make_async_copy(queries.at[:, lanes(me, WIDE)], qbuf.at[me], local_sem.at[2]),
    )
    for copy in own:
        copy.start()
    for step in range(1, PEERS):
        q_copy(step).start()

    def sub_ref(plane, core_, sub):
        return kv.at[plane, :, pl.ds(part(core_, fold if sub == 0 else 1 - fold), ROWS)]

    def ring_copy(way, hop, sub):
        plane = (z + (RING - (hop - 1) if way == 0 else hop - 1)) % RING
        ref = sub_ref(plane, core, sub)
        return remote(
            ref, ref, ring_send.at[way, hop, sub], ring_recv.at[way, hop, sub], up if way == 0 else down
        )

    def twin_copy(plane, sub):
        ref = sub_ref(plane, core, sub)
        return remote(ref, ref, twin_send.at[plane, sub], twin_recv.at[plane, sub], twin)

    y_ref = sub_ref(z, core, 0)
    y_copy = remote(y_ref, y_ref, y_send, y_recv, beside)

    for copy in own[:2]:
        copy.wait()
    for step in range(1, PEERS):
        for which in range(2):
            kv_copy(step, which).wait_recv()
    y_copy.start()
    ring_copy(0, 1, 0).start()
    ring_copy(1, 1, 0).start()
    twin_copy(z, 0).start()
    y_copy.wait_recv()
    ring_copy(0, 1, 1).start()
    ring_copy(1, 1, 1).start()
    twin_copy(z, 1).start()

    def item_q(i):
        return qbuf[:, :, i * HEAD_DIM : (i + 1) * HEAD_DIM].reshape(ROWS, HEAD_DIM)

    def query_position():
        row = lax.broadcasted_iota(jnp.int32, (ROWS, PLANE), 0)
        return token_position(row, core, fold)

    def token_position(index, core_, fold_):
        slot, xx = index // (4 * BLOCK), (index // BLOCK) % 4
        line = jnp.where(slot == 1, 3 - fold_, fold_)
        return line * ROWS + ((xx % 2) * 4 + (xx // 2) * 2 + core_) * BLOCK + index % BLOCK

    def key_position():
        index = lax.broadcasted_iota(jnp.int32, (ROWS, PLANE), 1)
        return token_position(index % ROWS, index // (2 * ROWS), (index // ROWS) % 2)

    scores = (score_a, score_b)

    def multiply(plane, i):
        scores[i % 2][...] = lax.dot_general(
            item_q(i), kv[plane, 0], TRANSPOSED, preferred_element_type=jnp.float32
        )

    def soften(plane, i, first):
        score = scores[i % 2][...]
        if first:
            score = jnp.where(query_position() >= key_position(), score, LOW)
        top = jnp.broadcast_to(jnp.max(score, axis=1, keepdims=True), (ROWS, HEAD_DIM))
        if not first:
            before = tops[i]
            top = jnp.maximum(before, top)
            rescale = jnp.exp2((before - top) * SCALE)
        weight = jnp.exp2((score - jnp.tile(top, (1, PLANE // HEAD_DIM))) * SCALE)
        tops[i] = top
        mixed = jnp.dot(weight.astype(jnp.bfloat16), kv[plane, 1], preferred_element_type=jnp.float32)
        partial = weight[:, :HEAD_DIM]
        for column in range(1, PLANE // HEAD_DIM):
            partial = partial + weight[:, column * HEAD_DIM : (column + 1) * HEAD_DIM]
        if first:
            acc[i], sums[i] = mixed, partial
        else:
            acc[i], sums[i] = acc[i] * rescale + mixed, sums[i] * rescale + partial

    def o_copy(step, piece):
        other, device = peer(step)
        columns = pl.ds(pl.multiple_of(me * WIDE + piece * PIECE, PIECE), PIECE)
        return remote(
            obuf.at[other, :, pl.ds(piece * PIECE, PIECE)], out.at[:, columns],
            o_send.at[step, piece], o_recv.at[step, piece], device,
        )

    def finish(i):
        total = jnp.sum(sums[i], axis=1, keepdims=True)
        result = (acc[i] / total).astype(jnp.bfloat16)
        obuf[:, :, i * HEAD_DIM : (i + 1) * HEAD_DIM] = result.reshape(PEERS, BLOCK, HEAD_DIM)
        if (i + 1) % (GROUP // PIECES) == 0:
            for step in range(1, PEERS):
                o_copy(step, i // (GROUP // PIECES)).start()

    def sweep(plane, first=False, last=False):
        multiply(plane, 0)
        for i in range(GROUP):
            if i + 1 < GROUP:
                multiply(plane, i + 1)
            soften(plane, i, first)
            if last:
                finish(i)

    twin_copy(z, 0).wait_recv()
    twin_copy(z, 1).wait_recv()
    own[2].wait()
    for step in range(1, PEERS):
        q_copy(step).wait_recv()
    sweep(z, first=True)

    def far(way, hop):
        return (z + (RING - hop if way == 0 else hop)) % RING

    for hop in (1, 2, 3):
        for sub in range(2):
            for way in range(2):
                ring_copy(way, hop, sub).wait_recv()
                if hop < 3 or way == sub:
                    ring_copy(way, hop + 1, sub).start()
                twin_copy(far(way, hop), sub).start()
        for way in range(2):
            plane = far(way, hop)
            twin_copy(plane, 0).wait_recv()
            twin_copy(plane, 1).wait_recv()

        def one(way, carry):
            plane = (z + jnp.where(way == 0, RING - hop, hop)) % RING

            @pl.when(plane < z)
            def _():
                sweep(plane)

            return carry

        lax.fori_loop(0, 2, one, 0)

    opposite = (z + 4) % RING
    for sub in range(2):
        ring_copy(sub, 4, sub).wait_recv()
        twin_copy(opposite, sub).start()
    for sub in range(2):
        twin_copy(opposite, sub).wait_recv()

    @pl.when(opposite < z)
    def _():
        sweep(opposite, last=True)

    @pl.when(opposite > z)
    def _():
        for i in range(GROUP):
            finish(i)

    own_out = pltpu.make_async_copy(obuf.at[me], out.at[:, lanes(me, WIDE)], local_sem.at[3])
    own_out.start()

    for step in range(1, PEERS):
        for which in range(2):
            kv_copy(step, which).wait_send()
        q_copy(step).wait_send()
    y_copy.wait_send()
    for way in range(2):
        for hop in (1, 2, 3, 4):
            for sub in range(2):
                if hop < 4 or way == sub:
                    ring_copy(way, hop, sub).wait_send()
    for plane in range(RING):
        for sub in range(2):
            twin_copy(plane, sub).wait_send()
    for piece in range(PIECES):
        for step in range(1, PEERS):
            o_copy(step, piece).wait()
    own_out.wait()


def on_device(queries, keys, values):
    anywhere = pl.BlockSpec(memory_space=pl.ANY)
    return pl.pallas_call(
        kernel,
        out_shape=jax.ShapeDtypeStruct(queries.shape, jnp.bfloat16),
        in_specs=[anywhere] * 3,
        out_specs=anywhere,
        scratch_shapes=[
            pltpu.VMEM((PEERS, BLOCK, WIDE), jnp.bfloat16),
            pltpu.VMEM((RING, 2, PLANE, HEAD_DIM), jnp.bfloat16),
            pltpu.VMEM((PEERS, BLOCK, WIDE), jnp.bfloat16),
            pltpu.VMEM((GROUP, ROWS, HEAD_DIM), jnp.float32),
            pltpu.VMEM((GROUP, ROWS, HEAD_DIM), jnp.float32),
            pltpu.VMEM((GROUP, ROWS, HEAD_DIM), jnp.float32),
            pltpu.VMEM((ROWS, PLANE), jnp.float32),
            pltpu.VMEM((ROWS, PLANE), jnp.float32),
            pltpu.SemaphoreType.DMA((4,)),
            pltpu.SemaphoreType.DMA((PEERS,)),
            pltpu.SemaphoreType.DMA((PEERS,)),
            pltpu.SemaphoreType.DMA((2, PEERS)),
            pltpu.SemaphoreType.DMA((2, PEERS)),
            pltpu.SemaphoreType.DMA,
            pltpu.SemaphoreType.DMA,
            pltpu.SemaphoreType.DMA((2, 5, 2)),
            pltpu.SemaphoreType.DMA((2, 5, 2)),
            pltpu.SemaphoreType.DMA((RING, 2)),
            pltpu.SemaphoreType.DMA((RING, 2)),
            pltpu.SemaphoreType.DMA((PEERS, PIECES)),
            pltpu.SemaphoreType.DMA((PEERS, PIECES)),
        ],
        compiler_params=pltpu.CompilerParams(
            collective_id=0, has_side_effects=True, vmem_limit_bytes=48 * 2**20
        ),
    )(queries, keys, values)


def solution(mesh):
    spec = P(("seq", "head"), None)
    return jax.shard_map(on_device, mesh=mesh, in_specs=(spec,) * 3, out_specs=spec, check_vma=False)
```

time: 776 us -> 59.8 us (0.08)
  the two profiles are of different devices: /device:TPU:248 before, /device:TPU:1 now
where the time goes in v1:
time: 59.8 us; the launch traced here: 59.3 us
  Pallas kernels  55.8 us (93%)
  local copies, waits for them, and re-layouts  3.51 us (6%)
    pallas_call x1, Pallas kernels, on_device(): pl.pallas_call(kernel, out_shape=jax.ShapeDtypeStruct(queries.shape, jnp....  55.8 us
    unnamed x7, local copies, waits for them, and re-layouts  3.51 us

profile of v1, /device:TPU:1, one launch (start us, length us, event | category | flops | bytes accessed | tf_op | source)
XLA Modules:
  0.0 59.3 jit_solution(312274899657631250)
XLA Ops:
  0.0 0.0 copy-start
  0.0 1.0 %copy-done = bf16[32,8192]{1,0:T(8,128)(2,1)S(1)} copy-done((bf16[32,8192]{1,0:T(8,128)(2,1)S(1)}, bf16[32,8192]{1,0:T(8,128)(2,1)}, u32[]{:S(2)}) %copy-start) | copy-done | bytes 524312
  1.0 0.0 copy-start.1
  1.0 0.8 %copy-done.1 = bf16[32,1024]{1,0:T(8,128)(2,1)S(1)} copy-done((bf16[32,1024]{1,0:T(8,128)(2,1)S(1)}, bf16[32,1024]{1,0:T(8,128)(2,1)}, u32[]{:S(2)}) %copy-start.1) | copy-done | bytes 65560
  1.9 0.0 copy-start.2
  1.9 0.8 %copy-done.2 = bf16[32,1024]{1,0:T(8,128)(2,1)S(1)} copy-done((bf16[32,1024]{1,0:T(8,128)(2,1)S(1)}, bf16[32,1024]{1,0:T(8,128)(2,1)}, u32[]{:S(2)}) %copy-start.2) | copy-done | bytes 65560
  2.7 55.8 %shard_map.37 = bf16[32,8192]{1,0:T(8,128)(2,1)S(1)} custom-call(bf16[32,8192]{1,0:T(8,128)(2,1)S(1)} %copy-done, bf16[32,1024]{1,0:T(8,128)(2,1)S(1)} %copy-done.1, bf16[32,1024]{1,0:T(8,128)(2,1)S(1)} %copy-done.2), custom_call_target="tpu_custom_call" | custom-call | tf_op jit(solution)/shard_map/pallas_call | solution.py:266
  58.5 0.8 %copy.5 = bf16[32,8192]{1,0:T(8,128)(2,1)} copy(bf16[32,8192]{1,0:T(8,128)(2,1)S(1)} %shard_map.37) | data formatting | bytes 1048576
Async XLA Ops:
  0.0 1.0 %copy-start = (bf16[32,8192]{1,0:T(8,128)(2,1)S(1)}, bf16[32,8192]{1,0:T(8,128)(2,1)}, u32[]{:S(2)}) copy-start(bf16[32,8192]{1,0:T(8,128)(2,1)} %queries.1) | copy-start | bytes 1572868
  1.0 0.8 %copy-start.1 = (bf16[32,1024]{1,0:T(8,128)(2,1)S(1)}, bf16[32,1024]{1,0:T(8,128)(2,1)}, u32[]{:S(2)}) copy-start(bf16[32,1024]{1,0:T(8,128)(2,1)} %keys.1) | copy-start | bytes 196612
  1.9 0.8 %copy-start.2 = (bf16[32,1024]{1,0:T(8,128)(2,1)S(1)}, bf16[32,1024]{1,0:T(8,128)(2,1)}, u32[]{:S(2)}) copy-start(bf16[32,1024]{1,0:T(8,128)(2,1)} %values.1) | copy-start | bytes 196612

commit v2 on v0

v2 whole, which is shorter than its diff:
```python
import jax
import jax.numpy as jnp
import numpy as np
from jax import lax
from jax.experimental import pallas as pl
from jax.experimental.pallas import tpu as pltpu
from jax.sharding import PartitionSpec as P

MESH = pl.DeviceIdType.MESH
HEAD_DIM = 128
GROUP = 8
WIDE = GROUP * HEAD_DIM
BLOCK = 32
PLANES = 8
SIDE = 4
ROWS = GROUP * BLOCK
KEYS = SIDE * SIDE * 2 * BLOCK
PHASES = ((0, 1), (1, 3), (3, 5), (5, 7), (7, 8))
SCALE = np.float32(HEAD_DIM**-0.5 / np.log(2.0))
LOW = np.float32(-1e30)
TRANSPOSED = (((1,), (1,)), ((), ()))
NEAR_FIRST = (1, 7, 2, 6, 3, 5, 4)


def kernel(
    queries, keys, values, out,
    qbuf, kv, obuf, tops, sums, acc, score_a, score_b,
    local_sem, q_send, q_recv, kv_send, kv_recv, one_send, one_recv, two_send, two_recv,
    twin_send, twin_recv, o_send, o_recv,
):
    seq, head = lax.axis_index("seq"), lax.axis_index("head")
    x_lo, y, z = seq % 2, (seq // 2) % 4, seq // 8
    x_hi, core = head // 2, head % 2
    x, place = x_hi * 2 + x_lo, x_lo * 2 + x_hi

    def at(x_, y_, z_, core_):
        return ((z_ * 4 + y_) * 2 + x_ % 2, (x_ // 2) * 2 + core_)

    def along_z(step):
        other = (z + step) % PLANES
        return other, at(x, y, other, core)

    def along_x(step):
        return at((x + step) % SIDE, y, z, core)

    def along_y(step):
        return at(x, (y + step) % SIDE, z, core)

    twin = at(x, y, z, 1 - core)

    barrier = pltpu.get_barrier_semaphore()
    greeted = [along_z(step)[1] for step in NEAR_FIRST]
    greeted += [along(step) for along in (along_x, along_y) for step in (1, 2, 3)] + [twin]
    for device in greeted:
        pl.semaphore_signal(barrier, inc=1, device_id=device, device_id_type=MESH)
    pl.semaphore_wait(barrier, len(greeted))

    def lanes(index, width):
        return pl.ds(pl.multiple_of(index * width, width), width)

    def remote(src, dst, send, recv, device):
        return pltpu.make_async_remote_copy(
            src_ref=src, dst_ref=dst, send_sem=send, recv_sem=recv, device_id=device, device_id_type=MESH
        )

    def kv_copy(step, which):
        other, device = along_z(step)
        return remote(
            (keys, values)[which].at[:, lanes(other, HEAD_DIM)], kv.at[z, which, core, y, place],
            kv_send.at[which, step], kv_recv.at[which, step], device,
        )

    def q_copy(step):
        other, device = along_z(step)
        return remote(queries.at[:, lanes(other, WIDE)], qbuf.at[z], q_send.at[step], q_recv.at[step], device)

    for step in NEAR_FIRST:
        for which in range(2):
            kv_copy(step, which).start()
    own = (
        pltpu.make_async_copy(keys.at[:, lanes(z, HEAD_DIM)], kv.at[z, 0, core, y, place], local_sem.at[0]),
        pltpu.make_async_copy(values.at[:, lanes(z, HEAD_DIM)], kv.at[z, 1, core, y, place], local_sem.at[1]),
        pltpu.make_async_copy(queries.at[:, lanes(z, WIDE)], qbuf.at[z], local_sem.at[2]),
    )
    for copy in own:
        copy.start()
    for step in NEAR_FIRST:
        q_copy(step).start()

    def planes(phase):
        start, stop = PHASES[phase]
        return pl.ds(start, stop - start)

    def one_copy(phase, which, step):
        ref = kv.at[planes(phase), which, core, y, place]
        device = (along_x, along_y)[which](step)
        return remote(ref, ref, one_send.at[phase, which, step], one_recv.at[phase, which, step], device)

    def two_copy(phase, which, step):
        ref = (kv.at[planes(phase), 0, core, y], kv.at[planes(phase), 1, core, :, place])[which]
        device = (along_y, along_x)[which](step)
        return remote(ref, ref, two_send.at[phase, which, step], two_recv.at[phase, which, step], device)

    def twin_copy(phase):
        ref = kv.at[planes(phase), :, core]
        return remote(ref, ref, twin_send.at[phase], twin_recv.at[phase], twin)

    six = [(which, step) for step in (1, 3, 2) for which in range(2)]

    def spread(phase):
        for which, step in six:
            one_copy(phase, which, step).wait_recv()
        for which, step in six:
            two_copy(phase, which, step).start()

    def pair(phase):
        for which, step in six:
            two_copy(phase, which, step).wait_recv()
        twin_copy(phase).start()

    def slice_of(plane):
        block = qbuf[plane]
        return jnp.concatenate([block[:, h * HEAD_DIM : (h + 1) * HEAD_DIM] for h in range(GROUP)], axis=0)

    def visible(plane, key_plane):
        row = lax.broadcasted_iota(jnp.int32, (ROWS, KEYS), 0)
        index = lax.broadcasted_iota(jnp.int32, (ROWS, KEYS), 1)
        query = (y * SIDE + place) * (2 * BLOCK) + core * BLOCK + row % BLOCK
        key = (index // BLOCK) % (SIDE * SIDE) * (2 * BLOCK) + index // (KEYS // 2) * BLOCK + index % BLOCK
        return query + (plane - key_plane) * KEYS >= key

    scores = (score_a, score_b)

    def multiply(item, n):
        plane, key_plane, _ = item
        scores[n % 2][...] = lax.dot_general(
            slice_of(plane), kv[key_plane, 0].reshape(KEYS, HEAD_DIM), TRANSPOSED,
            preferred_element_type=jnp.float32,
        )

    def soften(item, n):
        plane, key_plane, masked = item
        first = key_plane == 0
        score = scores[n % 2][...]
        if masked:
            score = jnp.where(visible(plane, key_plane), score, LOW)
        top = jnp.broadcast_to(jnp.max(score, axis=1, keepdims=True), (ROWS, HEAD_DIM))
        if not first:
            before = tops[plane]
            top = jnp.maximum(before, top)
            rescale = jnp.exp2((before - top) * SCALE)
        weight = jnp.exp2((score - jnp.tile(top, (1, KEYS // HEAD_DIM))) * SCALE)
        tops[plane] = top
        mixed = jnp.dot(
            weight.astype(jnp.bfloat16), kv[key_plane, 1].reshape(KEYS, HEAD_DIM),
            preferred_element_type=jnp.float32,
        )
        partial = weight[:, :HEAD_DIM]
        for column in range(1, KEYS // HEAD_DIM):
            partial = partial + weight[:, column * HEAD_DIM : (column + 1) * HEAD_DIM]
        if first:
            acc[plane], sums[plane] = mixed, partial
        else:
            acc[plane], sums[plane] = acc[plane] * rescale + mixed, sums[plane] * rescale + partial

    def sweep(items):
        multiply(items[0], 0)
        for n, item in enumerate(items):
            if n + 1 < len(items):
                multiply(items[n + 1], n + 1)
            soften(item, n)
            if isinstance(item[0], int) and item[0] == item[1]:
                finish(item[0])

    def o_copy(plane):
        return remote(
            obuf.at[plane], out.at[:, lanes(z, WIDE)], o_send.at[plane], o_recv.at[z], at(x, y, plane, core)
        )

    own_out = pltpu.make_async_copy(obuf.at[z], out.at[:, lanes(z, WIDE)], local_sem.at[3])

    def finish(plane):
        total = jnp.sum(sums[plane], axis=1, keepdims=True)
        result = (acc[plane] / total).astype(jnp.bfloat16)
        for h in range(GROUP):
            obuf[plane, :, h * HEAD_DIM : (h + 1) * HEAD_DIM] = result[h * BLOCK : (h + 1) * BLOCK]
        pl.when(plane != z)(lambda: o_copy(plane).start())
        pl.when(plane == z)(lambda: own_out.start())

    for copy in own[:2]:
        copy.wait()
    for step in NEAR_FIRST:
        for which in range(2):
            kv_copy(step, which).wait_recv()
    for phase in range(len(PHASES)):
        for which, step in six:
            one_copy(phase, which, step).start()
    def follow(phase):
        for which, step in six:
            two_copy(phase - 1, which, step).wait_send()
        spread(phase)

    def steps(*near):
        return [((z + step) % PLANES, 0, True) for step in near]

    def rest(phase):
        start, stop = PHASES[phase]
        return [
            (plane, key_plane, plane == key_plane)
            for plane in range(start, PLANES)
            for key_plane in range(start, min(plane + 1, stop))
        ]

    spread(0)
    follow(1)
    pair(0)
    follow(2)
    own[2].wait()
    for step in (1, 7, 2, 6):
        q_copy(step).wait_recv()
    twin_copy(0).wait_recv()
    sweep(steps(0, 1, 7, 2, 6))
    pair(1)
    follow(3)
    for step in (3, 5, 4):
        q_copy(step).wait_recv()
    sweep(steps(3, 5, 4))
    finish(0)
    twin_copy(1).wait_recv()
    items = rest(1)
    sweep(items[:7])
    pair(2)
    follow(4)
    sweep(items[7:])
    pair(3)
    twin_copy(2).wait_recv()
    sweep(rest(2))
    pair(4)
    twin_copy(3).wait_recv()
    sweep(rest(3))
    twin_copy(4).wait_recv()
    sweep(rest(4))

    for which, step in six:
        two_copy(4, which, step).wait_send()
    for step in NEAR_FIRST:
        for which in range(2):
            kv_copy(step, which).wait_send()
        q_copy(step).wait_send()
    for phase in range(len(PHASES)):
        for which, step in six:
            one_copy(phase, which, step).wait_send()
        twin_copy(phase).wait_send()
    own_out.wait()
    for plane in range(PLANES):

        @pl.when(plane != z)
        def _():
            o_copy(plane).wait_send()
            ref = out.at[:, lanes(plane, WIDE)]
            remote(ref, ref, o_send.at[plane], o_recv.at[plane], at(x, y, plane, core)).wait_recv()


def on_device(queries, keys, values):
    anywhere = pl.BlockSpec(memory_space=pl.ANY)
    return pl.pallas_call(
        kernel,
        out_shape=jax.ShapeDtypeStruct(queries.shape, jnp.bfloat16),
        in_specs=[anywhere] * 3,
        out_specs=anywhere,
        scratch_shapes=[
            pltpu.VMEM((PLANES, BLOCK, WIDE), jnp.bfloat16),
            pltpu.VMEM((PLANES, 2, 2, SIDE, SIDE, BLOCK, HEAD_DIM), jnp.bfloat16),
            pltpu.VMEM((PLANES, BLOCK, WIDE), jnp.bfloat16),
            pltpu.VMEM((PLANES, ROWS, HEAD_DIM), jnp.float32),
            pltpu.VMEM((PLANES, ROWS, HEAD_DIM), jnp.float32),
            pltpu.VMEM((PLANES, ROWS, HEAD_DIM), jnp.float32),
            pltpu.VMEM((ROWS, KEYS), jnp.float32),
            pltpu.VMEM((ROWS, KEYS), jnp.float32),
            pltpu.SemaphoreType.DMA((4,)),
            pltpu.SemaphoreType.DMA((PLANES,)),
            pltpu.SemaphoreType.DMA((PLANES,)),
            pltpu.SemaphoreType.DMA((2, PLANES)),
            pltpu.SemaphoreType.DMA((2, PLANES)),
            pltpu.SemaphoreType.DMA((len(PHASES), 2, SIDE)),
            pltpu.SemaphoreType.DMA((len(PHASES), 2, SIDE)),
            pltpu.SemaphoreType.DMA((len(PHASES), 2, SIDE)),
            pltpu.SemaphoreType.DMA((len(PHASES), 2, SIDE)),
            pltpu.SemaphoreType.DMA((len(PHASES),)),
            pltpu.SemaphoreType.DMA((len(PHASES),)),
            pltpu.SemaphoreType.DMA((PLANES,)),
            pltpu.SemaphoreType.DMA((PLANES,)),
        ],
        compiler_params=pltpu.CompilerParams(
            collective_id=0, has_side_effects=True, vmem_limit_bytes=60 * 2**20
        ),
    )(queries, keys, values)


def solution(mesh):
    spec = P(("seq", "head"), None)
    return jax.shard_map(on_device, mesh=mesh, in_specs=(spec,) * 3, out_specs=spec, check_vma=False)
```

time: 776 us -> 55.2 us (0.07)
  the two profiles are of different devices: /device:TPU:248 before, /device:TPU:1 now
where the time goes in v2:
time: 55.2 us; the launch traced here: 55 us
  Pallas kernels  53.1 us (96%)
  local copies, waits for them, and re-layouts  1.87 us (3%)
    pallas_call x1, Pallas kernels, on_device(): pl.pallas_call(kernel, out_shape=jax.ShapeDtypeStruct(queries.shape, jnp....  53.1 us
    unnamed x1, local copies, waits for them, and re-layouts  1.87 us

profile of v2, /device:TPU:1, one launch (start us, length us, event | category | flops | bytes accessed | tf_op | source)
XLA Modules:
  0.0 55.0 jit_solution(12285129782134270637)
XLA Ops:
  0.0 53.1 %shard_map.37 = bf16[32,8192]{1,0:T(8,128)(2,1)} custom-call(bf16[32,8192]{1,0:T(8,128)(2,1)} %queries.1, bf16[32,1024]{1,0:T(8,128)(2,1)} %keys.1, bf16[32,1024]{1,0:T(8,128)(2,1)} %values.1), custom_call_target="tpu_custom_call" | custom-call | tf_op jit(solution)/shard_map/pallas_call | solution.py:266
  53.1 1.9 %copy.5 = bf16[32,8192]{1,0:T(8,128)(2,1)} copy(bf16[32,8192]{1,0:T(8,128)(2,1)} %shard_map.37) | data formatting | bytes 1048576

commit v3 on v2

--- a/solution.py
+++ b/solution.py
@@ -203,13 +203,8 @@
     def steps(*near):
         return [((z + step) % PLANES, 0, True) for step in near]
 
-    def rest(phase):
-        start, stop = PHASES[phase]
-        return [
-            (plane, key_plane, plane == key_plane)
-            for plane in range(start, PLANES)
-            for key_plane in range(start, min(plane + 1, stop))
-        ]
+    def pairs(plane, start, stop):
+        return [(plane, key_plane, plane == key_plane) for key_plane in range(start, stop)]
 
     spread(0)
     follow(1)
@@ -227,19 +222,20 @@
     sweep(steps(3, 5, 4))
     finish(0)
     twin_copy(1).wait_recv()
-    items = rest(1)
-    sweep(items[:7])
+    sweep(pairs(1, 1, 2) + pairs(2, 1, 3) + pairs(3, 1, 3))
     pair(2)
     follow(4)
-    sweep(items[7:])
+    sweep(pairs(4, 1, 3) + pairs(5, 1, 3))
+    twin_copy(2).wait_recv()
+    sweep(pairs(3, 3, 4) + pairs(4, 3, 5) + pairs(5, 3, 4))
     pair(3)
-    twin_copy(2).wait_recv()
-    sweep(rest(2))
+    sweep(pairs(5, 4, 5) + pairs(6, 1, 3))
+    twin_copy(3).wait_recv()
+    sweep(pairs(5, 5, 6) + pairs(6, 3, 7))
     pair(4)
-    twin_copy(3).wait_recv()
-    sweep(rest(3))
+    sweep(pairs(7, 1, 7))
     twin_copy(4).wait_recv()
-    sweep(rest(4))
+    sweep(pairs(7, 7, 8))
 
     for which, step in six:
         two_copy(4, which, step).wait_send()

time: 55.2 us -> 53.9 us (0.976)
  Pallas kernels: 53.1 us -> 51.9 us
    pallas_call x1, Pallas kernels: 53.1 us -> 51.9 us  [on_device(): pl.pallas_call(kernel, out_shape=jax.ShapeDtypeStruct(queries.shape, jnp....]
where the time goes in v3:
time: 53.9 us; the launch traced here: 53.8 us
  Pallas kernels  51.9 us (96%)
  local copies, waits for them, and re-layouts  1.87 us (3%)
    pallas_call x1, Pallas kernels, on_device(): pl.pallas_call(kernel, out_shape=jax.ShapeDtypeStruct(queries.shape, jnp....  51.9 us
    unnamed x1, local copies, waits for them, and re-layouts  1.87 us

profile of v3, /device:TPU:1, one launch (start us, length us, event | category | flops | bytes accessed | tf_op | source)
XLA Modules:
  0.0 53.8 jit_solution(7219036137328546603)
XLA Ops:
  0.0 51.9 %shard_map.37 = bf16[32,8192]{1,0:T(8,128)(2,1)} custom-call(bf16[32,8192]{1,0:T(8,128)(2,1)} %queries.1, bf16[32,1024]{1,0:T(8,128)(2,1)} %keys.1, bf16[32,1024]{1,0:T(8,128)(2,1)} %values.1), custom_call_target="tpu_custom_call" | custom-call | tf_op jit(solution)/shard_map/pallas_call | solution.py:262
  51.9 1.9 %copy.5 = bf16[32,8192]{1,0:T(8,128)(2,1)} copy(bf16[32,8192]{1,0:T(8,128)(2,1)} %shard_map.37) | data formatting | bytes 1048576

commit v4 on v3

--- a/solution.py
+++ b/solution.py
@@ -91,10 +91,11 @@
         start, stop = PHASES[phase]
         return pl.ds(start, stop - start)
 
-    def one_copy(phase, which, step):
-        ref = kv.at[planes(phase), which, core, y, place]
+    def one_copy(part, which, step):
+        some = planes(0) if part == 0 else pl.ds(PHASES[1][0], PLANES - PHASES[1][0])
+        ref = kv.at[some, which, core, y, place]
         device = (along_x, along_y)[which](step)
-        return remote(ref, ref, one_send.at[phase, which, step], one_recv.at[phase, which, step], device)
+        return remote(ref, ref, one_send.at[part, which, step], one_recv.at[part, which, step], device)
 
     def two_copy(phase, which, step):
         ref = (kv.at[planes(phase), 0, core, y], kv.at[planes(phase), 1, core, :, place])[which]
@@ -108,8 +109,9 @@
     six = [(which, step) for step in (1, 3, 2) for which in range(2)]
 
     def spread(phase):
-        for which, step in six:
-            one_copy(phase, which, step).wait_recv()
+        if phase < 2:
+            for which, step in six:
+                one_copy(phase, which, step).wait_recv()
         for which, step in six:
             two_copy(phase, which, step).start()
 
@@ -192,9 +194,9 @@
     for step in NEAR_FIRST:
         for which in range(2):
             kv_copy(step, which).wait_recv()
-    for phase in range(len(PHASES)):
-        for which, step in six:
-            one_copy(phase, which, step).start()
+    for part in range(2):
+        for which, step in six:
+            one_copy(part, which, step).start()
     def follow(phase):
         for which, step in six:
             two_copy(phase - 1, which, step).wait_send()
@@ -243,9 +245,10 @@
         for which in range(2):
             kv_copy(step, which).wait_send()
         q_copy(step).wait_send()
+    for part in range(2):
+        for which, step in six:
+            one_copy(part, which, step).wait_send()
     for phase in range(len(PHASES)):
-        for which, step in six:
-            one_copy(phase, which, step).wait_send()
         twin_copy(phase).wait_send()
     own_out.wait()
     for plane in range(PLANES):
@@ -278,8 +281,8 @@
             pltpu.SemaphoreType.DMA((PLANES,)),
             pltpu.SemaphoreType.DMA((2, PLANES)),
             pltpu.SemaphoreType.DMA((2, PLANES)),
-            pltpu.SemaphoreType.DMA((len(PHASES), 2, SIDE)),
-            pltpu.SemaphoreType.DMA((len(PHASES), 2, SIDE)),
+            pltpu.SemaphoreType.DMA((2, 2, SIDE)),
+            pltpu.SemaphoreType.DMA((2, 2, SIDE)),
             pltpu.SemaphoreType.DMA((len(PHASES), 2, SIDE)),
             pltpu.SemaphoreType.DMA((len(PHASES), 2, SIDE)),
             pltpu.SemaphoreType.DMA((len(PHASES),)),

time: 53.9 us -> 53.5 us (level)
  no operation moved by 1% of the time
where the time goes in v4:
time: 53.5 us; the launch traced here: 53.4 us
  Pallas kernels  51.5 us (96%)
  local copies, waits for them, and re-layouts  1.87 us (3%)
    pallas_call x1, Pallas kernels, on_device(): pl.pallas_call(kernel, out_shape=jax.ShapeDtypeStruct(queries.shape, jnp....  51.5 us
    unnamed x1, local copies, waits for them, and re-layouts  1.87 us

profile of v4, /device:TPU:1, one launch (start us, length us, event | category | flops | bytes accessed | tf_op | source)
XLA Modules:
  0.0 53.4 jit_solution(6641348777274809068)
XLA Ops:
  0.0 51.5 %shard_map.37 = bf16[32,8192]{1,0:T(8,128)(2,1)} custom-call(bf16[32,8192]{1,0:T(8,128)(2,1)} %queries.1, bf16[32,1024]{1,0:T(8,128)(2,1)} %keys.1, bf16[32,1024]{1,0:T(8,128)(2,1)} %values.1), custom_call_target="tpu_custom_call" | custom-call | tf_op jit(solution)/shard_map/pallas_call | solution.py:265
  51.5 1.9 %copy.5 = bf16[32,8192]{1,0:T(8,128)(2,1)} copy(bf16[32,8192]{1,0:T(8,128)(2,1)} %shard_map.37) | data formatting | bytes 1048576

commit v5 on v4

--- a/solution.py
+++ b/solution.py
@@ -48,35 +48,9 @@
 
     twin = at(x, y, z, 1 - core)
 
-    barrier = pltpu.get_barrier_semaphore()
-    greeted = [along_z(step)[1] for step in NEAR_FIRST]
-    greeted += [along(step) for along in (along_x, along_y) for step in (1, 2, 3)] + [twin]
-    for device in greeted:
-        pl.semaphore_signal(barrier, inc=1, device_id=device, device_id_type=MESH)
-    pl.semaphore_wait(barrier, len(greeted))
-
     def lanes(index, width):
         return pl.ds(pl.multiple_of(index * width, width), width)
 
-    def remote(src, dst, send, recv, device):
-        return pltpu.make_async_remote_copy(
-            src_ref=src, dst_ref=dst, send_sem=send, recv_sem=recv, device_id=device, device_id_type=MESH
-        )
-
-    def kv_copy(step, which):
-        other, device = along_z(step)
-        return remote(
-            (keys, values)[which].at[:, lanes(other, HEAD_DIM)], kv.at[z, which, core, y, place],
-            kv_send.at[which, step], kv_recv.at[which, step], device,
-        )
-
-    def q_copy(step):
-        other, device = along_z(step)
-        return remote(queries.at[:, lanes(other, WIDE)], qbuf.at[z], q_send.at[step], q_recv.at[step], device)
-
-    for step in NEAR_FIRST:
-        for which in range(2):
-            kv_copy(step, which).start()
     own = (
         pltpu.make_async_copy(keys.at[:, lanes(z, HEAD_DIM)], kv.at[z, 0, core, y, place], local_sem.at[0]),
         pltpu.make_async_copy(values.at[:, lanes(z, HEAD_DIM)], kv.at[z, 1, core, y, place], local_sem.at[1]),
@@ -84,6 +58,33 @@
     )
     for copy in own:
         copy.start()
+
+    barrier = pltpu.get_barrier_semaphore()
+    greeted = [along_z(step)[1] for step in NEAR_FIRST]
+    greeted += [along(step) for along in (along_x, along_y) for step in (1, 2, 3)] + [twin]
+    for device in greeted:
+        pl.semaphore_signal(barrier, inc=1, device_id=device, device_id_type=MESH)
+    pl.semaphore_wait(barrier, len(greeted))
+
+    def remote(src, dst, send, recv, device):
+        return pltpu.make_async_remote_copy(
+            src_ref=src, dst_ref=dst, send_sem=send, recv_sem=recv, device_id=device, device_id_type=MESH
+        )
+
+    def kv_copy(step, which):
+        other, device = along_z(step)
+        return remote(
+            (keys, values)[which].at[:, lanes(other, HEAD_DIM)], kv.at[z, which, core, y, place],
+            kv_send.at[which, step], kv_recv.at[which, step], device,
+        )
+
+    def q_copy(step):
+        other, device = along_z(step)
+        return remote(queries.at[:, lanes(other, WIDE)], qbuf.at[z], q_send.at[step], q_recv.at[step], device)
+
+    for step in NEAR_FIRST:
+        for which in range(2):
+            kv_copy(step, which).start()
     for step in NEAR_FIRST:
         q_copy(step).start()
 

time: 53.5 us -> 53.5 us (level)
  no operation moved by 1% of the time
where the time goes in v5:
time: 53.5 us; the launch traced here: 53.4 us
  Pallas kernels  51.5 us (96%)
  local copies, waits for them, and re-layouts  1.87 us (3%)
    pallas_call x1, Pallas kernels, on_device(): pl.pallas_call(kernel, out_shape=jax.ShapeDtypeStruct(queries.shape, jnp....  51.5 us
    unnamed x1, local copies, waits for them, and re-layouts  1.87 us

profile of v5, /device:TPU:1, one launch (start us, length us, event | category | flops | bytes accessed | tf_op | source)
XLA Modules:
  0.0 53.4 jit_solution(2801528940007982260)
XLA Ops:
  0.0 51.5 %shard_map.37 = bf16[32,8192]{1,0:T(8,128)(2,1)} custom-call(bf16[32,8192]{1,0:T(8,128)(2,1)} %queries.1, bf16[32,1024]{1,0:T(8,128)(2,1)} %keys.1, bf16[32,1024]{1,0:T(8,128)(2,1)} %values.1), custom_call_target="tpu_custom_call" | custom-call | tf_op jit(solution)/shard_map/pallas_call | solution.py:266
  51.5 1.9 %copy.5 = bf16[32,8192]{1,0:T(8,128)(2,1)} copy(bf16[32,8192]{1,0:T(8,128)(2,1)} %shard_map.37) | data formatting | bytes 1048576
